TPU v7x, 32 devices: a whole 2x2x4 slice. The times are simulated.
32 devices in a mesh: grp: 2 (over y), bx: 4 (over x, core), by: 4 (over z).
Axes of the slice: x: 2, y: 2, z: 4, core: 2. Of those that a mesh axis runs over, the one named last changes fastest.
Arguments:
- volume: bfloat16 [128, 64, 128], P(('grp', 'bx'), 'by'), parts along dimension 0, may hold values from -6 to 6
- labels: int32 [64, 32, 64], P(('grp', 'bx'), 'by'), parts along dimension 0, may hold values from 0 to 15
- depth_order: int32 [8, 4], P('grp'), parts along dimension 0, may hold values from 0 to 3, as said below
- view_shear: int32 [8], P('grp'), parts along dimension 0, may hold values from -2 to 2
- tf_index: int32 [16], replicated, may hold values from 0 to 255
- color_table: float32 [256, 4], replicated, may hold values from 0.1 to 1
Outputs:
- image: float32 [8, 4, 64, 128], P(('grp', 'bx'), None, 'by'), parts along dimension 0
There are 2 independent parts, one for each index of `grp`. A program takes and returns all parts, laid end to end along the dimension named above; an argument that names none is the same for every part. Nothing has to cross between parts.
Inputs may be any that keep to these rules, and one draw needn't show every extreme that they name: `depth_order`: each row is 0, 1, ..., 3 in ascending or in descending order.
All inputs are finite; a program needn't handle non-finite values.
Results may differ from a plain program's by a relative error of at most 0.0003.
Values may be sent and summed in bfloat16 or wider, within the bound.
A program may use at most 64 MiB of HBM per device.

v0:
```python
import jax
import jax.numpy as jnp
from jax import lax
from jax.sharding import PartitionSpec as P


def padded_2(block, sides, width):
    for axis, dim in sides:
        count = lax.axis_size(axis)
        forward = [(i, i + 1) for i in range(count - 1)]
        backward = [(target, source) for source, target in forward]
        low = lax.ppermute(
            lax.slice_in_dim(block, block.shape[dim] - width, None, axis=dim), axis, forward
        )
        high = lax.ppermute(lax.slice_in_dim(block, 0, width, axis=dim), axis, backward)
        block = jnp.concatenate([low, block, high], axis=dim)
    return block


def shade(padded, labels, tf_index, color_table, x_cells):
    dens = padded.astype(jnp.float32)
    centre = dens[1:-1, 1:-1]
    grad_x = (dens[2:, 1:-1] - dens[:-2, 1:-1]) * 0.5
    grad_y = (dens[1:-1, 2:] - dens[1:-1, :-2]) * 0.5
    zpad = jnp.pad(centre, ((0, 0), (0, 0), (1, 1)))
    grad_z = (zpad[:, :, 2:] - zpad[:, :, :-2]) * 0.5
    grad_sq = grad_x * grad_x + grad_y * grad_y + grad_z * grad_z
    edge = grad_sq / (1.0 + grad_sq)
    classes = tf_index.shape[0]
    table_rows = color_table.shape[0]
    pick = (tf_index[:, None] == jnp.arange(table_rows, dtype=jnp.int32)[None, :]).astype(
        jnp.float32
    )
    class_color = jnp.dot(pick, color_table, precision=lax.Precision.HIGHEST)
    member = (labels[None] == jnp.arange(classes, dtype=jnp.int32)[:, None, None, None]).astype(
        jnp.float32
    )
    coarse = jnp.einsum("cxyz,ck->kxyz", member, class_color, precision=lax.Precision.HIGHEST)
    chans, half_x, half_y, half_z = coarse.shape
    finer = jnp.broadcast_to(
        coarse[:, :, None, :, None, :, None], (chans, half_x, 2, half_y, 2, half_z, 2)
    )
    finer = finer.reshape(chans, 2 * half_x, 2 * half_y, 2 * half_z)
    tau = 6.0 / x_cells * jax.nn.sigmoid(2.0 * centre) * finer[3] * (0.25 + edge)
    alpha = -jnp.expm1(-tau)
    emission = finer[:3] * (0.5 + 0.5 * jnp.tanh(centre))
    return jnp.concatenate([alpha[None] * emission, tau[None]], 0)


def on_device(volume, labels, depth_order, view_shear, tf_index, color_table):
    brick_x, brick_y, cells_z = volume.shape
    bricks = lax.axis_size("bx")
    x_cells = brick_x * bricks
    my_index = lax.axis_index("bx")
    views = depth_order.shape[0]
    per_dev = views // bricks
    padded = padded_2(volume, (("bx", 0), ("by", 1)), 1)
    field = shade(padded, labels, tf_index, color_table, x_cells)
    pad_z = cells_z // 4
    field_pad = jnp.pad(field, ((0, 0), (0, 0), (0, 0), (pad_z, pad_z)))
    slab_x = my_index * brick_x + jnp.arange(brick_x, dtype=jnp.int32)

    def one_view(view):
        shear = view_shear[view]
        ascending = depth_order[view, 0] == 0
        offsets = shear * slab_x * cells_z // (8 * x_cells)
        sheared = jax.vmap(
            lambda plane, offset: lax.dynamic_slice_in_dim(plane, pad_z - offset, cells_z, 2),
            in_axes=(1, 0),
            out_axes=1,
        )(field_pad, offsets)
        depth = sheared[3]
        running = jnp.cumsum(depth, 0)
        total = running[-1]
        before = jnp.where(ascending, running - depth, total[None] - running)
        color = jnp.sum(jnp.exp(-before)[None] * sheared[:3], 1)
        return jnp.concatenate([color, total[None]], 0)

    partials = lax.map(one_view, jnp.arange(views, dtype=jnp.int32))
    received = lax.all_to_all(partials[:, None], "bx", split_axis=0, concat_axis=1, tiled=True)
    owned = my_index * per_dev + jnp.arange(per_dev, dtype=jnp.int32)
    ascending = jnp.take(depth_order[:, 0], owned) == 0
    depth = received[:, :, 3]
    running = jnp.cumsum(depth, 1)
    total = running[:, -1]
    before = jnp.where(ascending[:, None, None, None], running - depth, total[:, None] - running)
    color = jnp.sum(jnp.exp(-before)[:, :, None] * received[:, :, :3], 1)
    return jnp.concatenate([color, (-jnp.expm1(-total))[:, None]], 1)


def solution(mesh):
    return jax.shard_map(
        on_device,
        mesh=mesh,
        in_specs=(
            P(("grp", "bx"), "by", None),
            P(("grp", "bx"), "by", None),
            P("grp", None),
            P("grp"),
            P(),
            P(),
        ),
        out_specs=P(("grp", "bx"), None, "by", None),
        check_vma=False,
    )
```

profile of v0, /device:TPU:0, one launch (start us, length us, event | category | flops | bytes accessed | tf_op | source)
XLA Modules:
  0.0 141.1 jit_solution(7051120777551149247)
XLA Ops:
  0.0 0.0 copy-start
  0.0 0.7 fusion.38
  0.7 2.3 %collective-permute-start = (bf16[1,16,128]{2,1,0:T(8,128)(2,1)S(1)}, bf16[1,16,128]{2,1,0:T(8,128)(2,1)S(1)}, u32[]{:S(2)}, u32[]{:S(2)}) collective-permute-start(bf16[1,16,128]{2,1,0:T(8,128)(2,1)S(1)} %get-tuple-element.161), channel_id=1, source_target_pairs={{0,4},{4,8},{8,12},{1,5},{5,9},{9,13},{2,6},{6,10},{10,14},{3,7},{... | collective-permute-start | bytes 12296 | tf_op jit(solution)/shard_map/ppermute | solution.py:12
  3.1 1.3 collective-permute-start.1
  4.4 0.0 copy-done
  4.4 0.8 convolution_bitcast_fusion
  5.2 0.0 collective-permute-done
  5.2 0.9 constant_dynamic-update-slice_fusion.1
  6.1 2.1 %collective-permute-done.1 = bf16[1,16,128]{2,1,0:T(8,128)(2,1)S(1)} collective-permute-done((bf16[1,16,128]{2,1,0:T(8,128)(2,1)S(1)}, bf16[1,16,128]{2,1,0:T(8,128)(2,1)S(1)}, u32[]{:S(2)}, u32[]{:S(2)}) %collective-permute-start.1) | collective-permute-done | bytes 4128 | tf_op jit(solution)/shard_map/ppermute | solution.py:15
  8.3 3.5 %collective-permute-start.2 = (bf16[18,1,128]{2,1,0:T(2,128)(2,1)S(1)}, bf16[18,1,128]{2,1,0:T(2,128)(2,1)S(1)}, u32[]{:S(2)}, u32[]{:S(2)}) collective-permute-start(bf16[18,1,128]{2,1,0:T(2,128)(2,1)S(1)} %get-tuple-element.158), channel_id=1, source_target_pairs={{0,1},{1,2},{2,3},{4,5},{5,6},{6,7},{8,9},{9,10},{10,11},{12,13},{... | collective-permute-start | bytes 13832 | tf_op jit(solution)/shard_map/ppermute | solution.py:12
  11.8 1.3 collective-permute-start.3
  13.1 1.0 fusion.13
  14.2 3.8 %broadcast_in_dim.55 = f32[8,2,8,2,64,2]{5,4,3,2,1,0:T(8,128)} broadcast(f32[8,8,64]{2,1,0:T(8,128)S(1)} %bitcast.115), dimensions={0,2,4} | broadcast | bytes 147456 | tf_op jit(solution)/shard_map/broadcast_in_dim | solution.py:40
  18.0 6.9 %broadcast_in_dim.56 = f32[16,16,128]{2,1,0:T(8,128)S(1)} reshape(f32[8,2,8,2,64,2]{5,4,3,2,1,0:T(8,128)} %broadcast_in_dim.55) | data formatting | bytes 262144 | tf_op jit(solution)/shard_map/broadcast_in_dim | solution.py:40
  24.9 9.0 %broadcast_in_dim.57 = f32[3,8,2,8,2,64,2]{6,5,4,3,2,1,0:T(8,128)} broadcast(f32[3,8,8,64]{3,2,1,0:T(8,128)S(1)} %copy.19), dimensions={0,1,3,5} | broadcast | bytes 442368 | tf_op jit(solution)/shard_map/broadcast_in_dim | solution.py:40
  33.9 18.3 %slice.92 = f32[3,16,16,128]{3,2,1,0:T(8,128)S(1)} reshape(f32[3,8,2,8,2,64,2]{6,5,4,3,2,1,0:T(8,128)} %broadcast_in_dim.57) | data formatting | bytes 786432 | tf_op jit(solution)/shard_map/slice | solution.py:46
  52.2 0.0 collective-permute-done.2
  52.2 0.0 collective-permute-done.3
  52.3 0.2 exponential-minus-one_negate_fusion
  52.5 0.1 multiply_multiply_fusion
  52.6 3.4 %copy.22 = f32[4,16,16,128]{2,0,1,3:T(4,128)} copy(f32[4,16,16,128]{3,2,1,0:T(8,128)S(1)} %pad_maximum_fusion) | data formatting | bytes 1048576
  56.0 0.0 copy-start.1
  56.0 0.0 copy-start.2
  56.0 7.3 %pad.13.clone = f32[4,16,16,192]{2,0,1,3:T(4,128)} pad(f32[4,16,16,128]{2,0,1,3:T(4,128)} %copy.22, f32[]{:T(128)} %constant.112.clone.1), padding=0_0x0_0x0_0x32_32 | pad | bytes 1310724 | tf_op jit(solution)/shard_map/jit(_pad)/pad | solution.py:60
  63.3 0.0 copy-done.1
  63.3 0.0 copy-done.2
  63.3 68.5 %while.14 = (s32[]{:T(128)}, f32[4,4,16,128]{3,2,1,0:T(8,128)}, s32[4]{0:T(128)S(1)}, s32[4,4]{1,0:T(4,128)S(1)}, f32[4,16,16,192]{2,0,1,3:T(4,128)}, /*index=5*...) while((s32[]{:T(128)}, f32[4,4,16,128]{3,2,1,0:T(8,128)}, s32[4]{0:T(128)S(1)}, ...), condition=%wide.region_3.4_spmd.clone, body=%wide.region_0.3_spmd.clone.sunk | while | flops 821686 | bytes 3400689 | solution.py:79
  63.3 0.6 dynamic_slice.25
  65.6 0.6 dynamic_slice.26
  66.1 0.6 or_bitcast_fusion.2
  66.7 8.4 %gather_fusion = f32[16,4,16,128]{2,1,3,0:T(4,128)} fusion(f32[16,4,16,192]{2,1,0,3:T(4,128)} %bitcast.109, s32[16]{0:T(128)S(1)} %or_bitcast_fusion.2), kind=kCustom, calls=%fused_computation.clone.clone.1 | custom fusion | bytes 1048832 | tf_op jit(solution)/shard_map/while/body/eval_jaxpr/vmap()/gather | solution.py:68
  75.1 3.4 %copy.24 = f32[16,4,16,128]{3,2,0,1:T(8,128)S(1)} copy(f32[16,4,16,128]{2,1,3,0:T(4,128)} %gather_fusion) | data formatting | bytes 1048576 | tf_op jit(solution)/shard_map/while/body/eval_jaxpr/vmap()/gather | solution.py:68
  78.6 0.5 fusion.50
  79.1 0.6 fusion.51
  79.8 0.6 fusion.53
  80.4 0.6 dynamic_slice.25
  82.7 0.6 dynamic_slice.26
  83.3 0.6 or_bitcast_fusion.2
  83.8 8.4 %gather_fusion = f32[16,4,16,128]{2,1,3,0:T(4,128)} fusion(f32[16,4,16,192]{2,1,0,3:T(4,128)} %bitcast.109, s32[16]{0:T(128)S(1)} %or_bitcast_fusion.2), kind=kCustom, calls=%fused_computation.clone.clone.1 | custom fusion | bytes 1048832 | tf_op jit(solution)/shard_map/while/body/eval_jaxpr/vmap()/gather | solution.py:68
  92.3 3.4 %copy.24 = f32[16,4,16,128]{3,2,0,1:T(8,128)S(1)} copy(f32[16,4,16,128]{2,1,3,0:T(4,128)} %gather_fusion) | data formatting | bytes 1048576 | tf_op jit(solution)/shard_map/while/body/eval_jaxpr/vmap()/gather | solution.py:68
  95.8 0.5 fusion.50
  96.3 0.6 fusion.51
  96.9 0.6 fusion.53
  97.5 0.6 dynamic_slice.25
  99.8 0.6 dynamic_slice.26
  100.4 0.6 or_bitcast_fusion.2
  101.0 8.4 %gather_fusion = f32[16,4,16,128]{2,1,3,0:T(4,128)} fusion(f32[16,4,16,192]{2,1,0,3:T(4,128)} %bitcast.109, s32[16]{0:T(128)S(1)} %or_bitcast_fusion.2), kind=kCustom, calls=%fused_computation.clone.clone.1 | custom fusion | bytes 1048832 | tf_op jit(solution)/shard_map/while/body/eval_jaxpr/vmap()/gather | solution.py:68
  109.4 3.4 %copy.24 = f32[16,4,16,128]{3,2,0,1:T(8,128)S(1)} copy(f32[16,4,16,128]{2,1,3,0:T(4,128)} %gather_fusion) | data formatting | bytes 1048576 | tf_op jit(solution)/shard_map/while/body/eval_jaxpr/vmap()/gather | solution.py:68
  112.9 0.5 fusion.50
  113.4 0.6 fusion.51
  114.1 0.6 fusion.53
  114.7 0.6 dynamic_slice.25
  116.9 0.6 dynamic_slice.26
  117.5 0.6 or_bitcast_fusion.2
  118.1 8.4 %gather_fusion = f32[16,4,16,128]{2,1,3,0:T(4,128)} fusion(f32[16,4,16,192]{2,1,0,3:T(4,128)} %bitcast.109, s32[16]{0:T(128)S(1)} %or_bitcast_fusion.2), kind=kCustom, calls=%fused_computation.clone.clone.1 | custom fusion | bytes 1048832 | tf_op jit(solution)/shard_map/while/body/eval_jaxpr/vmap()/gather | solution.py:68
  126.5 3.4 %copy.24 = f32[16,4,16,128]{3,2,0,1:T(8,128)S(1)} copy(f32[16,4,16,128]{2,1,3,0:T(4,128)} %gather_fusion) | data formatting | bytes 1048576 | tf_op jit(solution)/shard_map/while/body/eval_jaxpr/vmap()/gather | solution.py:68
  130.0 0.5 fusion.50
  130.5 0.6 fusion.51
  131.2 0.6 fusion.53
  131.8 4.0 %all-to-all-start = ((f32[4,1,4,16,128]{4,3,2,1,0:T(8,128)}), f32[4,1,4,16,128]{4,3,2,1,0:T(8,128)S(1)}, u32[]{:S(2)}, u32[]{:S(2)}) async-start(f32[4,1,4,16,128]{4,3,2,1,0:T(8,128)} %bitcast.8), calls=%async_computation | async-start | bytes 262144 | tf_op jit(solution)/shard_map/all_to_all | solution.py:80
  135.8 0.5 fusion.39
  136.9 3.5 %all-to-all-done = f32[4,1,4,16,128]{4,3,2,1,0:T(8,128)S(1)} async-done(((f32[4,1,4,16,128]{4,3,2,1,0:T(8,128)}), f32[4,1,4,16,128]{4,3,2,1,0:T(8,128)S(1)}, u32[]{:S(2)}, u32[]{:S(2)}) %all-to-all-start) | async-done | bytes 131104 | tf_op jit(solution)/shard_map/all_to_all | solution.py:80
  140.5 0.6 pad_maximum_fusion.1
  (26 shorter events, 0.5 us)
Async XLA Ops:
  0.0 4.4 %copy-start = (f32[256,4]{0,1:T(4,128)S(1)}, f32[256,4]{0,1:T(4,128)}, u32[]{:S(2)}) copy-start(f32[256,4]{0,1:T(4,128)} %param.13) | copy-start | bytes 12292
  0.7 4.5 %collective-permute-start = (bf16[1,16,128]{2,1,0:T(8,128)(2,1)S(1)}, bf16[1,16,128]{2,1,0:T(8,128)(2,1)S(1)}, u32[]{:S(2)}, u32[]{:S(2)}) collective-permute-start(bf16[1,16,128]{2,1,0:T(8,128)(2,1)S(1)} %get-tuple-element.161), channel_id=1, source_target_pairs={{0,4},{4,8},{8,12},{1,5},{5,9},{9,13},{2,6},{6,10},{10,14},{3,7},{... | collective-permute-start | bytes 12296 | tf_op jit(solution)/shard_map/ppermute | solution.py:12
  3.1 5.2 %collective-permute-start.1 = (bf16[1,16,128]{2,1,0:T(8,128)(2,1)S(1)}, bf16[1,16,128]{2,1,0:T(8,128)(2,1)S(1)}, u32[]{:S(2)}, u32[]{:S(2)}) collective-permute-start(bf16[1,16,128]{2,1,0:T(8,128)(2,1)S(1)} %get-tuple-element.160), channel_id=1, source_target_pairs={{4,0},{8,4},{12,8},{5,1},{9,5},{13,9},{6,2},{10,6},{14,10},{7,3},{... | collective-permute-start | bytes 12296 | tf_op jit(solution)/shard_map/ppermute | solution.py:15
  8.3 43.9 %collective-permute-start.2 = (bf16[18,1,128]{2,1,0:T(2,128)(2,1)S(1)}, bf16[18,1,128]{2,1,0:T(2,128)(2,1)S(1)}, u32[]{:S(2)}, u32[]{:S(2)}) collective-permute-start(bf16[18,1,128]{2,1,0:T(2,128)(2,1)S(1)} %get-tuple-element.158), channel_id=1, source_target_pairs={{0,1},{1,2},{2,3},{4,5},{5,6},{6,7},{8,9},{9,10},{10,11},{12,13},{... | collective-permute-start | bytes 13832 | tf_op jit(solution)/shard_map/ppermute | solution.py:12
  11.8 40.5 %collective-permute-start.3 = (bf16[18,1,128]{2,1,0:T(2,128)(2,1)S(1)}, bf16[18,1,128]{2,1,0:T(2,128)(2,1)S(1)}, u32[]{:S(2)}, u32[]{:S(2)}) collective-permute-start(bf16[18,1,128]{2,1,0:T(2,128)(2,1)S(1)} %get-tuple-element.159), channel_id=1, source_target_pairs={{1,0},{2,1},{3,2},{5,4},{6,5},{7,6},{9,8},{10,9},{11,10},{13,12},{... | collective-permute-start | bytes 13832 | tf_op jit(solution)/shard_map/ppermute | solution.py:15
  56.0 7.3 %copy-start.1 = (s32[4,4]{1,0:T(4,128)S(1)}, s32[4,4]{1,0:T(4,128)}, u32[]{:S(2)}) copy-start(s32[4,4]{1,0:T(4,128)} %param.10) | copy-start | bytes 196
  56.0 7.3 %copy-start.2 = (s32[4]{0:T(128)S(1)}, s32[4]{0:T(128)}, u32[]{:S(2)}) copy-start(s32[4]{0:T(128)} %param.11) | copy-start | bytes 52
  131.8 8.6 %all-to-all-start = ((f32[4,1,4,16,128]{4,3,2,1,0:T(8,128)}), f32[4,1,4,16,128]{4,3,2,1,0:T(8,128)S(1)}, u32[]{:S(2)}, u32[]{:S(2)}) async-start(f32[4,1,4,16,128]{4,3,2,1,0:T(8,128)} %bitcast.8), calls=%async_computation | async-start | bytes 262144 | tf_op jit(solution)/shard_map/all_to_all | solution.py:80
where the time goes:
time: 142 us; the launch traced here: 141 us
  local copies, waits for them, and re-layouts  102 us (72%)
  starting transfers between devices  12.4 us (9%)
  other arithmetic  11 us (8%)
  loops' own time  6.97 us (5%)
  waiting for transfers between devices  5.63 us (4%)
  matrix products  1.87 us (1%)
    gather x8, local copies, waits for them, and re-layouts, one_view(): lax.dynamic_slice_in_dim(plane, pad_z - offset, cells_z, 2)  47.5 us
    broadcast_in_dim x3, local copies, waits for them, and re-layouts, shade(): jnp.broadcast_to(coarse[:, :, None, :, None, :, None], (chans, half_x, 2,...  19.7 us
    slice x2, local copies, waits for them, and re-layouts, shade(): emission = finer[:3] * (0.5 + 0.5 * jnp.tanh(centre))  18.3 us
    pad x1, local copies, waits for them, and re-layouts, on_device(): field_pad = jnp.pad(field, ((0, 0), (0, 0), (0, 0), (pad_z, pad_z)))  7.26 us
    another operation x1, loops' own time, on_device(): partials = lax.map(one_view, jnp.arange(views, dtype=jnp.int32))  6.97 us
    ppermute x2, starting transfers between devices, padded_2(): lax.ppermute(lax.slice_in_dim(block, block.shape[dim] - width, None, axis...  5.83 us
    unnamed x9, local copies, waits for them, and re-layouts  4.24 us
    all_to_all x1, starting transfers between devices, on_device(): lax.all_to_all(partials[:, None], 'bx', split_axis=0, concat_axis=1, tile...  3.99 us
  transfers between devices with their start and end apart: 5, of which 2 were waited for; matrix products, arithmetic and copies ran while one was open for 29% of the time, Pallas kernels for 0%

commit v1 on v0

v1 whole, which is shorter than its diff:
```python
import functools
import math

import jax
import jax.numpy as jnp
from jax import lax
from jax.experimental import pallas as pl
from jax.experimental.pallas import tpu as pltpu
from jax.sharding import PartitionSpec as P

MESH = pl.DeviceIdType.MESH


def one_minus_exp(depth):
    series = 1.0 - depth * (1.0 / 6.0)
    for term in (5.0, 4.0, 3.0, 2.0):
        series = 1.0 - depth * (1.0 / term) * series
    return jnp.where(depth < 0.125, depth * series, 1.0 - jnp.exp(-depth))


def render(
    bricks,
    columns,
    vol_ref,
    lab_ref,
    order_ref,
    shear_ref,
    tf_ref,
    color_ref,
    out_ref,
    plane_ref,
    edge_ref,
    row_ref,
    rgbo_ref,
    field_ref,
    part_ref,
    got_ref,
    halo_send,
    halo_recv,
    part_send,
    part_recv,
):
    brick_x, brick_y, cells_z = vol_ref.shape
    half_x, half_y, half_z = lab_ref.shape
    views = order_ref.shape[0]
    per_dev = views // bricks
    x_cells = brick_x * bricks
    me = lax.axis_index("bx")
    col = lax.axis_index("by")
    has_left, has_right = me > 0, me < bricks - 1
    has_up, has_down = col > 0, col < columns - 1

    barrier = pltpu.get_barrier_semaphore()
    for step in range(1, bricks):
        other = lax.rem(me + step, bricks)
        pl.semaphore_signal(barrier, inc=1, device_id={"bx": other}, device_id_type=MESH)

    @pl.when(has_up)
    def _():
        pl.semaphore_signal(barrier, inc=1, device_id={"by": col - 1}, device_id_type=MESH)

    @pl.when(has_down)
    def _():
        pl.semaphore_signal(barrier, inc=1, device_id={"by": col + 1}, device_id_type=MESH)

    for x in range(brick_x):
        plane = vol_ref[x].astype(jnp.float32)
        edge_ref[0, x : x + 1, :] = plane[brick_y - 1 :, :]
        edge_ref[1, x : x + 1, :] = plane[:1, :]

    amount = bricks - 1 + has_up.astype(jnp.int32) + has_down.astype(jnp.int32)
    pl.semaphore_wait(barrier, amount)

    def copy(index, src, dst, target):
        return pltpu.make_async_remote_copy(
            src_ref=src,
            dst_ref=dst,
            send_sem=halo_send.at[index],
            recv_sem=halo_recv.at[index],
            device_id=target,
            device_id_type=MESH,
        )

    halos = (
        (copy(0, vol_ref.at[brick_x - 1], plane_ref.at[0], {"bx": me + 1}), has_right, has_left, plane_ref, 0),
        (copy(1, vol_ref.at[0], plane_ref.at[1], {"bx": me - 1}), has_left, has_right, plane_ref, 1),
        (copy(2, edge_ref.at[0], row_ref.at[0], {"by": col + 1}), has_down, has_up, row_ref, 0),
        (copy(3, edge_ref.at[1], row_ref.at[1], {"by": col - 1}), has_up, has_down, row_ref, 1),
    )
    for halo, sends, receives, ref, slot in halos:
        pl.when(sends)(halo.start)

        @pl.when(jnp.logical_not(receives))
        def _():
            ref[slot] = jnp.zeros(ref.shape[1:], ref.dtype)

    lane = lax.broadcasted_iota(jnp.int32, (4, 128), 1)
    row_of = jnp.zeros((4, 128), jnp.int32)
    for index in range(tf_ref.shape[0]):
        row_of = jnp.where(lane == index, tf_ref[index], row_of)
    table = jnp.zeros((4, 128), jnp.float32)
    for base in range(0, color_ref.shape[1], 128):
        local = row_of - base
        inside = jnp.logical_and(local >= 0, local < 128)
        found = jnp.take_along_axis(
            color_ref[:, base : base + 128],
            jnp.where(inside, local, 0),
            axis=1,
            mode="promise_in_bounds",
        )
        table = jnp.where(inside, found, table)
    spread = (
        lax.broadcasted_iota(jnp.int32, (half_z, cells_z), 1) // 2
        == lax.broadcasted_iota(jnp.int32, (half_z, cells_z), 0)
    ).astype(jnp.bfloat16)
    rows, fine_rows = half_x * half_y, half_x * brick_y
    repeat = (
        lax.broadcasted_iota(jnp.int32, (fine_rows, rows), 0) // 2
        == lax.broadcasted_iota(jnp.int32, (fine_rows, rows), 1)
    ).astype(jnp.bfloat16)
    coarse = lab_ref[...].reshape(rows, half_z).astype(jnp.float32).astype(jnp.bfloat16)
    wide = jnp.dot(coarse, spread, preferred_element_type=jnp.float32).astype(jnp.bfloat16)
    fine = jnp.dot(repeat, wide, preferred_element_type=jnp.float32).astype(jnp.int32)
    for chan in range(4):
        entries = jnp.broadcast_to(table[chan : chan + 1], (fine_rows, 128))
        values = jnp.take_along_axis(entries, fine, axis=1, mode="promise_in_bounds")
        for x in range(half_x):
            rgbo_ref[x, chan] = values[x * brick_y : (x + 1) * brick_y]

    for halo, sends, receives, ref, slot in halos:
        pl.when(receives)(halo.wait_recv)

    row = lax.broadcasted_iota(jnp.int32, (brick_y, cells_z), 0)
    depth_lane = lax.broadcasted_iota(jnp.int32, (brick_y, cells_z), 1)

    def dens(x):
        if x < 0:
            return plane_ref[0].astype(jnp.float32)
        if x == brick_x:
            return plane_ref[1].astype(jnp.float32)
        return vol_ref[x].astype(jnp.float32)

    for x in range(brick_x):
        centre = dens(x)
        grad_x = (dens(x + 1) - dens(x - 1)) * 0.5
        above = jnp.where(row == 0, row_ref[0, x : x + 1, :], pltpu.roll(centre, 1, 0))
        below = jnp.where(
            row == brick_y - 1, row_ref[1, x : x + 1, :], pltpu.roll(centre, brick_y - 1, 0)
        )
        grad_y = (below - above) * 0.5
        before = jnp.where(depth_lane == 0, 0.0, pltpu.roll(centre, 1, 1))
        after = jnp.where(depth_lane == cells_z - 1, 0.0, pltpu.roll(centre, cells_z - 1, 1))
        grad_z = (after - before) * 0.5
        grad_sq = grad_x * grad_x + grad_y * grad_y + grad_z * grad_z
        edge = grad_sq / (1.0 + grad_sq)
        glow = 1.0 / (1.0 + jnp.exp(-2.0 * centre))
        tau = 6.0 / x_cells * glow * rgbo_ref[x // 2, 3] * (0.25 + edge)
        gain = one_minus_exp(tau) * glow
        for chan in range(3):
            field_ref[x, chan] = gain * rgbo_ref[x // 2, chan]
        field_ref[x, 3] = tau

    shrink = math.gcd(cells_z, 8 * x_cells)
    numer, denom = cells_z // shrink, 8 * x_cells // shrink

    def send_of(view):
        owner = lax.div(view, per_dev)
        local = lax.rem(view, per_dev)
        return owner, local, pltpu.make_async_remote_copy(
            src_ref=part_ref.at[view],
            dst_ref=got_ref.at[me, local],
            send_sem=part_send.at[view],
            recv_sem=part_recv.at[me, local],
            device_id={"bx": owner},
            device_id_type=MESH,
        )

    def one_view(step, carry):
        view = lax.rem((me + 1) * per_dev + step, views)
        ascending = order_ref[view, 0] == 0
        shear = shear_ref[view]
        color = [jnp.zeros((brick_y, cells_z), jnp.float32) for _ in range(3)]
        depth = jnp.zeros((brick_y, cells_z), jnp.float32)
        for index in range(brick_x):
            x = jnp.where(ascending, index, brick_x - 1 - index)
            scaled = shear * (me * brick_x + x) * numer
            ahead = lax.div(scaled + denom * cells_z, denom)
            turn = lax.rem(ahead, cells_z)
            source = depth_lane + (cells_z - ahead)
            inside = jnp.logical_and(source >= 0, source < cells_z)
            moved = pltpu.roll(field_ref[x].reshape(4 * brick_y, cells_z), turn, 1)
            seen = jnp.where(inside, jnp.exp(-depth), 0.0)
            for chan in range(3):
                color[chan] = color[chan] + seen * moved[chan * brick_y : (chan + 1) * brick_y]
            depth = depth + jnp.where(inside, moved[3 * brick_y :], 0.0)
        owner, local, send = send_of(view)

        @pl.when(owner != me)
        def _():
            for chan in range(3):
                part_ref[view, chan] = color[chan]
            part_ref[view, 3] = depth
            send.start()

        @pl.when(owner == me)
        def _():
            for chan in range(3):
                got_ref[me, local, chan] = color[chan]
            got_ref[me, local, 3] = depth

        return carry

    lax.fori_loop(0, views, one_view, 0)

    for step in range(1, bricks):
        source = lax.rem(me + step, bricks)
        for local in range(per_dev):
            pltpu.make_async_remote_copy(
                src_ref=part_ref.at[0],
                dst_ref=got_ref.at[source, local],
                send_sem=part_send.at[0],
                recv_sem=part_recv.at[source, local],
                device_id={"bx": source},
                device_id_type=MESH,
            ).wait_recv()

    for local in range(per_dev):
        ascending = order_ref[me * per_dev + local, 0] == 0
        color = [jnp.zeros((brick_y, cells_z), jnp.float32) for _ in range(3)]
        depth = jnp.zeros((brick_y, cells_z), jnp.float32)
        for index in range(bricks):
            brick = jnp.where(ascending, index, bricks - 1 - index)
            seen = jnp.exp(-depth)
            for chan in range(3):
                color[chan] = color[chan] + seen * got_ref[brick, local, chan]
            depth = depth + got_ref[brick, local, 3]
        for chan in range(3):
            out_ref[local, chan] = color[chan]
        out_ref[local, 3] = one_minus_exp(depth)

    for halo, sends, receives, ref, slot in halos:
        pl.when(sends)(halo.wait_send)
    for step in range(views - per_dev):
        view = lax.rem((me + 1) * per_dev + step, views)
        send_of(view)[2].wait_send()


def on_device(bricks, columns, volume, labels, depth_order, view_shear, tf_index, color_table):
    brick_x, brick_y, cells_z = volume.shape
    views = depth_order.shape[0]
    per_dev = views // bricks
    image = (4, brick_y, cells_z)
    vmem = pl.BlockSpec(memory_space=pltpu.VMEM)
    smem = pl.BlockSpec(memory_space=pltpu.SMEM)
    return pl.pallas_call(
        functools.partial(render, bricks, columns),
        out_shape=jax.ShapeDtypeStruct((per_dev,) + image, jnp.float32),
        in_specs=[vmem, vmem, smem, smem, smem, vmem],
        out_specs=vmem,
        scratch_shapes=[
            pltpu.VMEM((2, brick_y, cells_z), volume.dtype),
            pltpu.VMEM((2, brick_x, cells_z), jnp.float32),
            pltpu.VMEM((2, brick_x, cells_z), jnp.float32),
            pltpu.VMEM((labels.shape[0],) + image, jnp.float32),
            pltpu.VMEM((brick_x,) + image, jnp.float32),
            pltpu.VMEM((views,) + image, jnp.float32),
            pltpu.VMEM((bricks, per_dev) + image, jnp.float32),
            pltpu.SemaphoreType.DMA((4,)),
            pltpu.SemaphoreType.DMA((4,)),
            pltpu.SemaphoreType.DMA((views,)),
            pltpu.SemaphoreType.DMA((bricks, per_dev)),
        ],
        compiler_params=pltpu.CompilerParams(
            collective_id=0, has_side_effects=True, vmem_limit_bytes=32 * 2**20
        ),
    )(volume, labels, depth_order, view_shear, tf_index, color_table.T)


def solution(mesh):
    return jax.shard_map(
        functools.partial(on_device, mesh.shape["bx"], mesh.shape["by"]),
        mesh=mesh,
        in_specs=(
            P(("grp", "bx"), "by", None),
            P(("grp", "bx"), "by", None),
            P("grp", None),
            P("grp"),
            P(),
            P(),
        ),
        out_specs=P(("grp", "bx"), None, "by", None),
        check_vma=False,
    )
```

time: 142 us -> 15.7 us (0.11)
  local copies, waits for them, and re-layouts: 102 us -> 4.25 us
  starting transfers between devices: 12.4 us -> 0 us
  Pallas kernels: 0 us -> 11.2 us
  other arithmetic: 11 us -> 0 us
  loops' own time: 6.97 us -> 0 us
  waiting for transfers between devices: 5.63 us -> 0 us
  matrix products: 1.87 us -> 0 us
    gather x8 -> x0, local copies, waits for them, and re-layouts: 47.5 us -> none  [one_view(): lax.dynamic_slice_in_dim(plane, pad_z - offset, cells_z, 2)]
    broadcast_in_dim x3 -> x0, local copies, waits for them, and re-layouts: 19.7 us -> none  [shade(): jnp.broadcast_to(coarse[:, :, None, :, None, :, None], (chans, half_x, 2,...]
    slice x6 -> x0, local copies, waits for them, and re-layouts: 19.1 us -> none  [the longest x2 18.3 us: shade(): emission = finer[:3] * (0.5 + 0.5 * jnp.tanh(centre))]
    pallas_call x0 -> x1, Pallas kernels: none -> 11.2 us  [on_device(): pl.pallas_call(functools.partial(render, bricks, columns), out_shape=jax....]
    ppermute x4 -> x0, starting transfers between devices: 8.41 us -> none  [the longest x2 5.83 us: padded_2(): lax.ppermute(lax.slice_in_dim(block, block.shape[dim] - width, None, axis...]
    pad x1 -> x0, local copies, waits for them, and re-layouts: 7.26 us -> none  [on_device(): field_pad = jnp.pad(field, ((0, 0), (0, 0), (0, 0), (pad_z, pad_z)))]
    another operation x1 -> x0, loops' own time: 6.97 us -> none  [on_device(): partials = lax.map(one_view, jnp.arange(views, dtype=jnp.int32))]
    dynamic_slice x8 -> x0, local copies, waits for them, and re-layouts: 4.61 us -> none  [the longest x4 2.31 us: one_view(): shear = view_shear[view]]
  transfers between devices with their start and end apart: 5 -> 0, of which waited for: 2 -> 0; matrix products, arithmetic and copies ran while one was open for 29% -> 0% of each run, Pallas kernels for 0% -> 0%
where the time goes in v1:
time: 15.7 us; the launch traced here: 15.4 us
  Pallas kernels  11.2 us (71%)
  local copies, waits for them, and re-layouts  4.25 us (27%)
    pallas_call x1, Pallas kernels, on_device(): pl.pallas_call(functools.partial(render, bricks, columns), out_shape=jax....  11.2 us
    unnamed x13, local copies, waits for them, and re-layouts  4.25 us

profile of v1, /device:TPU:0, one launch (start us, length us, event | category | flops | bytes accessed | tf_op | source)
XLA Modules:
  0.0 15.4 jit_solution(4831830981522752669)
XLA Ops:
  0.0 0.0 copy-start.5
  0.0 0.0 copy-start.4
  0.0 0.7 %copy-done.5 = s32[16]{0:T(128)S(1)} copy-done((s32[16]{0:T(128)S(1)}, s32[16]{0:T(128)}, u32[]{:S(2)}) %copy-start.5) | copy-done | bytes 88
  0.7 0.0 copy-done.4
  0.7 0.0 copy-start
  0.7 0.8 %copy-done = bf16[16,16,128]{2,1,0:T(8,128)(2,1)S(1)} copy-done((bf16[16,16,128]{2,1,0:T(8,128)(2,1)S(1)}, bf16[16,16,128]{2,1,0:T(8,128)(2,1)}, u32[]{:S(2)}) %copy-start) | copy-done | bytes 65560
  1.5 0.0 copy-start.1
  1.5 0.8 %copy-done.1 = s32[8,8,64]{2,1,0:T(8,128)S(1)} copy-done((s32[8,8,64]{2,1,0:T(8,128)S(1)}, s32[8,8,64]{2,1,0:T(8,128)}, u32[]{:S(2)}) %copy-start.1) | copy-done | bytes 16408
  2.3 0.0 copy-start.2
  2.3 0.7 %copy-done.2 = f32[256,4]{0,1:T(4,128)S(1)} copy-done((f32[256,4]{0,1:T(4,128)S(1)}, f32[256,4]{0,1:T(4,128)}, u32[]{:S(2)}) %copy-start.2) | copy-done | bytes 4120
  3.0 0.0 copy-start.3
  3.0 0.7 %copy-done.3 = s32[4,4]{1,0:T(4,128)S(1)} copy-done((s32[4,4]{1,0:T(4,128)S(1)}, s32[4,4]{1,0:T(4,128)}, u32[]{:S(2)}) %copy-start.3) | copy-done | bytes 88
  3.6 11.2 %shard_map.64 = f32[1,4,16,128]{3,2,1,0:T(8,128)S(1)} custom-call(bf16[16,16,128]{2,1,0:T(8,128)(2,1)S(1)} %copy-done, s32[8,8,64]{2,1,0:T(8,128)S(1)} %copy-done.1, s32[4,4]{1,0:T(4,128)S(1)} %copy-done.3, s32[4]{0:T(128)S(1)} %copy-done.4, s32[16]{0:T(128)S(1)} %copy-done.5, f32[4,256]{1,0:T(4,128)S(1)} %bitcast.1), custom_call_target="tpu_custom_call" | custom-call | tf_op jit(solution)/shard_map/pallas_call | solution.py:255
  14.8 0.6 %copy.8 = f32[1,4,16,128]{3,2,1,0:T(8,128)} copy(f32[1,4,16,128]{3,2,1,0:T(8,128)S(1)} %shard_map.64) | data formatting | bytes 65536
Async XLA Ops:
  0.0 0.7 %copy-start.5 = (s32[16]{0:T(128)S(1)}, s32[16]{0:T(128)}, u32[]{:S(2)}) copy-start(s32[16]{0:T(128)} %tf_ref.1) | copy-start | bytes 196
  0.0 0.7 %copy-start.4 = (s32[4]{0:T(128)S(1)}, s32[4]{0:T(128)}, u32[]{:S(2)}) copy-start(s32[4]{0:T(128)} %shear_ref.1) | copy-start | bytes 52
  0.7 0.8 %copy-start = (bf16[16,16,128]{2,1,0:T(8,128)(2,1)S(1)}, bf16[16,16,128]{2,1,0:T(8,128)(2,1)}, u32[]{:S(2)}) copy-start(bf16[16,16,128]{2,1,0:T(8,128)(2,1)} %vol_ref.1) | copy-start | bytes 196612
  1.5 0.8 %copy-start.1 = (s32[8,8,64]{2,1,0:T(8,128)S(1)}, s32[8,8,64]{2,1,0:T(8,128)}, u32[]{:S(2)}) copy-start(s32[8,8,64]{2,1,0:T(8,128)} %lab_ref.1) | copy-start | bytes 49156
  2.3 0.7 %copy-start.2 = (f32[256,4]{0,1:T(4,128)S(1)}, f32[256,4]{0,1:T(4,128)}, u32[]{:S(2)}) copy-start(f32[256,4]{0,1:T(4,128)} %param.11) | copy-start | bytes 12292
  3.0 0.7 %copy-start.3 = (s32[4,4]{1,0:T(4,128)S(1)}, s32[4,4]{1,0:T(4,128)}, u32[]{:S(2)}) copy-start(s32[4,4]{1,0:T(4,128)} %order_ref.1) | copy-start | bytes 196

commit v2 on v1

--- a/solution.py
+++ b/solution.py
@@ -21,13 +21,21 @@
 def render(
     bricks,
     columns,
+    vol_hbm,
+    lab_hbm,
+    order_hbm,
+    shear_hbm,
+    tf_hbm,
+    color_hbm,
+    out_ref,
     vol_ref,
     lab_ref,
     order_ref,
     shear_ref,
     tf_ref,
     color_ref,
-    out_ref,
+    glow_ref,
+    grad_ref,
     plane_ref,
     edge_ref,
     row_ref,
@@ -39,6 +47,7 @@
     halo_recv,
     part_send,
     part_recv,
+    load_sem,
 ):
     brick_x, brick_y, cells_z = vol_ref.shape
     half_x, half_y, half_z = lab_ref.shape
@@ -63,6 +72,22 @@
     def _():
         pl.semaphore_signal(barrier, inc=1, device_id={"by": col + 1}, device_id_type=MESH)
 
+    pairs = (
+        (vol_hbm, vol_ref),
+        (lab_hbm, lab_ref),
+        (tf_hbm, tf_ref),
+        (color_hbm, color_ref),
+        (order_hbm, order_ref),
+        (shear_hbm, shear_ref),
+    )
+    loads = [
+        pltpu.make_async_copy(source, target, load_sem.at[index])
+        for index, (source, target) in enumerate(pairs)
+    ]
+    for load in loads:
+        load.start()
+    loads[0].wait()
+
     for x in range(brick_x):
         plane = vol_ref[x].astype(jnp.float32)
         edge_ref[0, x : x + 1, :] = plane[brick_y - 1 :, :]
@@ -93,6 +118,9 @@
         @pl.when(jnp.logical_not(receives))
         def _():
             ref[slot] = jnp.zeros(ref.shape[1:], ref.dtype)
+
+    for load in loads[1:]:
+        load.wait()
 
     lane = lax.broadcasted_iota(jnp.int32, (4, 128), 1)
     row_of = jnp.zeros((4, 128), jnp.int32)
@@ -127,9 +155,6 @@
         for x in range(half_x):
             rgbo_ref[x, chan] = values[x * brick_y : (x + 1) * brick_y]
 
-    for halo, sends, receives, ref, slot in halos:
-        pl.when(receives)(halo.wait_recv)
-
     row = lax.broadcasted_iota(jnp.int32, (brick_y, cells_z), 0)
     depth_lane = lax.broadcasted_iota(jnp.int32, (brick_y, cells_z), 1)
 
@@ -142,18 +167,33 @@
 
     for x in range(brick_x):
         centre = dens(x)
-        grad_x = (dens(x + 1) - dens(x - 1)) * 0.5
+        before = jnp.where(depth_lane == 0, 0.0, pltpu.roll(centre, 1, 1))
+        after = jnp.where(depth_lane == cells_z - 1, 0.0, pltpu.roll(centre, cells_z - 1, 1))
+        grad_z = (after - before) * 0.5
+        grad_sq = grad_z * grad_z
+        if 0 < x < brick_x - 1:
+            grad_x = (dens(x + 1) - dens(x - 1)) * 0.5
+            grad_sq = grad_sq + grad_x * grad_x
+        grad_ref[x] = grad_sq
+        glow_ref[x] = 1.0 / (1.0 + jnp.exp(-2.0 * centre))
+
+    for halo, sends, receives, ref, slot in halos:
+        pl.when(receives)(halo.wait_recv)
+
+    for x in range(brick_x):
+        centre = dens(x)
+        grad_sq = grad_ref[x]
+        if x == 0 or x == brick_x - 1:
+            grad_x = (dens(x + 1) - dens(x - 1)) * 0.5
+            grad_sq = grad_sq + grad_x * grad_x
         above = jnp.where(row == 0, row_ref[0, x : x + 1, :], pltpu.roll(centre, 1, 0))
         below = jnp.where(
             row == brick_y - 1, row_ref[1, x : x + 1, :], pltpu.roll(centre, brick_y - 1, 0)
         )
         grad_y = (below - above) * 0.5
-        before = jnp.where(depth_lane == 0, 0.0, pltpu.roll(centre, 1, 1))
-        after = jnp.where(depth_lane == cells_z - 1, 0.0, pltpu.roll(centre, cells_z - 1, 1))
-        grad_z = (after - before) * 0.5
-        grad_sq = grad_x * grad_x + grad_y * grad_y + grad_z * grad_z
+        grad_sq = grad_sq + grad_y * grad_y
         edge = grad_sq / (1.0 + grad_sq)
-        glow = 1.0 / (1.0 + jnp.exp(-2.0 * centre))
+        glow = glow_ref[x]
         tau = 6.0 / x_cells * glow * rgbo_ref[x // 2, 3] * (0.25 + edge)
         gain = one_minus_exp(tau) * glow
         for chan in range(3):
@@ -163,10 +203,33 @@
     shrink = math.gcd(cells_z, 8 * x_cells)
     numer, denom = cells_z // shrink, 8 * x_cells // shrink
 
+    def ahead_of(scaled):
+        if denom & (denom - 1) == 0:
+            return lax.shift_right_arithmetic(scaled, denom.bit_length() - 1) + cells_z
+        return lax.div(scaled + denom * cells_z, denom)
+
+    def composite(view):
+        ascending = order_ref[view, 0] == 0
+        shear = shear_ref[view]
+        color = [jnp.zeros((brick_y, cells_z), jnp.float32) for _ in range(3)]
+        depth = jnp.zeros((brick_y, cells_z), jnp.float32)
+        for index in range(brick_x):
+            x = jnp.where(ascending, index, brick_x - 1 - index)
+            ahead = ahead_of(shear * (me * brick_x + x) * numer)
+            turn = jnp.where(ahead >= cells_z, ahead - cells_z, ahead)
+            source = depth_lane + (cells_z - ahead)
+            inside = jnp.logical_and(source >= 0, source < cells_z)
+            moved = pltpu.roll(field_ref[x].reshape(4 * brick_y, cells_z), turn, 1)
+            seen = jnp.where(inside, jnp.exp(-depth), 0.0)
+            for chan in range(3):
+                color[chan] = color[chan] + seen * moved[chan * brick_y : (chan + 1) * brick_y]
+            depth = depth + jnp.where(inside, moved[3 * brick_y :], 0.0)
+        return color + [depth]
+
     def send_of(view):
         owner = lax.div(view, per_dev)
         local = lax.rem(view, per_dev)
-        return owner, local, pltpu.make_async_remote_copy(
+        return pltpu.make_async_remote_copy(
             src_ref=part_ref.at[view],
             dst_ref=got_ref.at[me, local],
             send_sem=part_send.at[view],
@@ -175,42 +238,20 @@
             device_id_type=MESH,
         )
 
-    def one_view(step, carry):
+    def other_view(step):
         view = lax.rem((me + 1) * per_dev + step, views)
-        ascending = order_ref[view, 0] == 0
-        shear = shear_ref[view]
-        color = [jnp.zeros((brick_y, cells_z), jnp.float32) for _ in range(3)]
-        depth = jnp.zeros((brick_y, cells_z), jnp.float32)
-        for index in range(brick_x):
-            x = jnp.where(ascending, index, brick_x - 1 - index)
-            scaled = shear * (me * brick_x + x) * numer
-            ahead = lax.div(scaled + denom * cells_z, denom)
-            turn = lax.rem(ahead, cells_z)
-            source = depth_lane + (cells_z - ahead)
-            inside = jnp.logical_and(source >= 0, source < cells_z)
-            moved = pltpu.roll(field_ref[x].reshape(4 * brick_y, cells_z), turn, 1)
-            seen = jnp.where(inside, jnp.exp(-depth), 0.0)
-            for chan in range(3):
-                color[chan] = color[chan] + seen * moved[chan * brick_y : (chan + 1) * brick_y]
-            depth = depth + jnp.where(inside, moved[3 * brick_y :], 0.0)
-        owner, local, send = send_of(view)
-
-        @pl.when(owner != me)
-        def _():
-            for chan in range(3):
-                part_ref[view, chan] = color[chan]
-            part_ref[view, 3] = depth
-            send.start()
-
-        @pl.when(owner == me)
-        def _():
-            for chan in range(3):
-                got_ref[me, local, chan] = color[chan]
-            got_ref[me, local, 3] = depth
-
-        return carry
-
-    lax.fori_loop(0, views, one_view, 0)
+        for chan, values in enumerate(composite(view)):
+            part_ref[view, chan] = values
+        send_of(view).start()
+
+    if views <= 4:
+        for step in range(views - per_dev):
+            other_view(step)
+    else:
+        pl.loop(0, views - per_dev)(other_view)
+    for local in range(per_dev):
+        for chan, values in enumerate(composite(me * per_dev + local)):
+            got_ref[me, local, chan] = values
 
     for step in range(1, bricks):
         source = lax.rem(me + step, bricks)
@@ -242,7 +283,7 @@
         pl.when(sends)(halo.wait_send)
     for step in range(views - per_dev):
         view = lax.rem((me + 1) * per_dev + step, views)
-        send_of(view)[2].wait_send()
+        send_of(view).wait_send()
 
 
 def on_device(bricks, columns, volume, labels, depth_order, view_shear, tf_index, color_table):
@@ -250,14 +291,22 @@
     views = depth_order.shape[0]
     per_dev = views // bricks
     image = (4, brick_y, cells_z)
-    vmem = pl.BlockSpec(memory_space=pltpu.VMEM)
-    smem = pl.BlockSpec(memory_space=pltpu.SMEM)
+    hbm = pl.BlockSpec(memory_space=pltpu.HBM)
+    colors = color_table.T
     return pl.pallas_call(
         functools.partial(render, bricks, columns),
         out_shape=jax.ShapeDtypeStruct((per_dev,) + image, jnp.float32),
-        in_specs=[vmem, vmem, smem, smem, smem, vmem],
-        out_specs=vmem,
+        in_specs=[hbm] * 6,
+        out_specs=pl.BlockSpec(memory_space=pltpu.VMEM),
         scratch_shapes=[
+            pltpu.VMEM(volume.shape, volume.dtype),
+            pltpu.VMEM(labels.shape, labels.dtype),
+            pltpu.SMEM(depth_order.shape, depth_order.dtype),
+            pltpu.SMEM(view_shear.shape, view_shear.dtype),
+            pltpu.SMEM(tf_index.shape, tf_index.dtype),
+            pltpu.VMEM(colors.shape, colors.dtype),
+            pltpu.VMEM(volume.shape, jnp.float32),
+            pltpu.VMEM(volume.shape, jnp.float32),
             pltpu.VMEM((2, brick_y, cells_z), volume.dtype),
             pltpu.VMEM((2, brick_x, cells_z), jnp.float32),
             pltpu.VMEM((2, brick_x, cells_z), jnp.float32),
@@ -269,11 +318,12 @@
             pltpu.SemaphoreType.DMA((4,)),
             pltpu.SemaphoreType.DMA((views,)),
             pltpu.SemaphoreType.DMA((bricks, per_dev)),
+            pltpu.SemaphoreType.DMA((6,)),
         ],
         compiler_params=pltpu.CompilerParams(
-            collective_id=0, has_side_effects=True, vmem_limit_bytes=32 * 2**20
+            collective_id=0, has_side_effects=True
         ),
-    )(volume, labels, depth_order, view_shear, tf_index, color_table.T)
+    )(volume, labels, depth_order, view_shear, tf_index, colors)
 
 
 def solution(mesh):

time: 15.7 us -> 12.6 us (0.80)
  local copies, waits for them, and re-layouts: 4.25 us -> 1.38 us
  Pallas kernels: 11.2 us -> 11 us
    unnamed x13 -> x1, local copies, waits for them, and re-layouts: 4.25 us -> 1.38 us
where the time goes in v2:
time: 12.6 us; the launch traced here: 12.4 us
  Pallas kernels  11 us (87%)
  local copies, waits for them, and re-layouts  1.38 us (11%)
    pallas_call x1, Pallas kernels, on_device(): pl.pallas_call(functools.partial(render, bricks, columns), out_shape=jax....  11 us
    unnamed x1, local copies, waits for them, and re-layouts  1.38 us

profile of v2, /device:TPU:0, one launch (start us, length us, event | category | flops | bytes accessed | tf_op | source)
XLA Modules:
  0.0 12.4 jit_solution(11219596006211919265)
XLA Ops:
  0.0 11.0 %shard_map.64 = f32[1,4,16,128]{3,2,1,0:T(8,128)} custom-call(bf16[16,16,128]{2,1,0:T(8,128)(2,1)} %vol_hbm.1, s32[8,8,64]{2,1,0:T(8,128)} %lab_hbm.1, s32[4,4]{1,0:T(4,128)} %order_hbm.1, s32[4]{0:T(128)} %shear_hbm.1, s32[16]{0:T(128)} %tf_hbm.1, f32[4,256]{1,0:T(4,128)} %bitcast.1), custom_call_target="tpu_custom_call" | custom-call | tf_op jit(solution)/shard_map/pallas_call | solution.py:296
  11.0 1.4 %copy.8 = f32[1,4,16,128]{3,2,1,0:T(8,128)} copy(f32[1,4,16,128]{3,2,1,0:T(8,128)} %shard_map.64) | data formatting | bytes 65536

commit v3 on v2

--- a/solution.py
+++ b/solution.py
@@ -86,13 +86,6 @@
     ]
     for load in loads:
         load.start()
-    loads[0].wait()
-
-    for x in range(brick_x):
-        plane = vol_ref[x].astype(jnp.float32)
-        edge_ref[0, x : x + 1, :] = plane[brick_y - 1 :, :]
-        edge_ref[1, x : x + 1, :] = plane[:1, :]
-
     amount = bricks - 1 + has_up.astype(jnp.int32) + has_down.astype(jnp.int32)
     pl.semaphore_wait(barrier, amount)
 
@@ -107,13 +100,22 @@
         )
 
     halos = (
-        (copy(0, vol_ref.at[brick_x - 1], plane_ref.at[0], {"bx": me + 1}), has_right, has_left, plane_ref, 0),
-        (copy(1, vol_ref.at[0], plane_ref.at[1], {"bx": me - 1}), has_left, has_right, plane_ref, 1),
+        (copy(0, vol_hbm.at[brick_x - 1], plane_ref.at[0], {"bx": me + 1}), has_right, has_left, plane_ref, 0),
+        (copy(1, vol_hbm.at[0], plane_ref.at[1], {"bx": me - 1}), has_left, has_right, plane_ref, 1),
         (copy(2, edge_ref.at[0], row_ref.at[0], {"by": col + 1}), has_down, has_up, row_ref, 0),
         (copy(3, edge_ref.at[1], row_ref.at[1], {"by": col - 1}), has_up, has_down, row_ref, 1),
     )
+    for halo, sends, receives, ref, slot in halos[:2]:
+        pl.when(sends)(halo.start)
+    loads[0].wait()
+    for x in range(brick_x):
+        plane = vol_ref[x].astype(jnp.float32)
+        edge_ref[0, x : x + 1, :] = plane[brick_y - 1 :, :]
+        edge_ref[1, x : x + 1, :] = plane[:1, :]
+    for halo, sends, receives, ref, slot in halos[2:]:
+        pl.when(sends)(halo.start)
+
     for halo, sends, receives, ref, slot in halos:
-        pl.when(sends)(halo.start)
 
         @pl.when(jnp.logical_not(receives))
         def _():
@@ -238,15 +240,23 @@
             device_id_type=MESH,
         )
 
+    def view_at(step):
+        turn = lax.div(step, per_dev)
+        local = lax.rem(step, per_dev)
+        pair, core = lax.div(me, 2), lax.rem(me, 2)
+        pair = lax.rem(pair + 1 + lax.div(turn, 2), bricks // 2)
+        core = jnp.where(turn == bricks - 2, 1 - core, lax.rem(core + turn, 2))
+        return (2 * pair + core) * per_dev + local
+
     def other_view(step):
-        view = lax.rem((me + 1) * per_dev + step, views)
+        view = view_at(step)
         for chan, values in enumerate(composite(view)):
             part_ref[view, chan] = values
         send_of(view).start()
 
     if views <= 4:
         for step in range(views - per_dev):
-            other_view(step)
+            other_view(jnp.int32(step))
     else:
         pl.loop(0, views - per_dev)(other_view)
     for local in range(per_dev):
@@ -282,8 +292,7 @@
     for halo, sends, receives, ref, slot in halos:
         pl.when(sends)(halo.wait_send)
     for step in range(views - per_dev):
-        view = lax.rem((me + 1) * per_dev + step, views)
-        send_of(view).wait_send()
+        send_of(view_at(jnp.int32(step))).wait_send()
 
 
 def on_device(bricks, columns, volume, labels, depth_order, view_shear, tf_index, color_table):
@@ -293,6 +302,10 @@
     image = (4, brick_y, cells_z)
     hbm = pl.BlockSpec(memory_space=pltpu.HBM)
     colors = color_table.T
+    arrays = [
+        pltpu.with_memory_space_constraint(array, pltpu.HBM)
+        for array in (volume, labels, depth_order, view_shear, tf_index, colors)
+    ]
     return pl.pallas_call(
         functools.partial(render, bricks, columns),
         out_shape=jax.ShapeDtypeStruct((per_dev,) + image, jnp.float32),
@@ -321,9 +334,9 @@
             pltpu.SemaphoreType.DMA((6,)),
         ],
         compiler_params=pltpu.CompilerParams(
-            collective_id=0, has_side_effects=True
+            collective_id=0, has_side_effects=True, vmem_limit_bytes=32 * 2**20
         ),
-    )(volume, labels, depth_order, view_shear, tf_index, colors)
+    )(*arrays)
 
 
 def solution(mesh):

time: 12.6 us -> 11 us (0.87)
  Pallas kernels: 11 us -> 10.2 us
  local copies, waits for them, and re-layouts: 1.38 us -> 0.62 us
    pallas_call x1, Pallas kernels: 11 us -> 10.2 us  [on_device(): pl.pallas_call(functools.partial(render, bricks, columns), out_shape=jax....]
    unnamed x1, local copies, waits for them, and re-layouts: 1.38 us -> 0.62 us
where the time goes in v3:
time: 11 us; the launch traced here: 10.9 us
  Pallas kernels  10.2 us (93%)
  local copies, waits for them, and re-layouts  0.62 us (6%)
    pallas_call x1, Pallas kernels, on_device(): pl.pallas_call(functools.partial(render, bricks, columns), out_shape=jax....  10.2 us
    unnamed x1, local copies, waits for them, and re-layouts  0.62 us

profile of v3, /device:TPU:0, one launch (start us, length us, event | category | flops | bytes accessed | tf_op | source)
XLA Modules:
  0.0 10.9 jit_solution(8735851224687719159)
XLA Ops:
  0.0 10.2 %shard_map.64 = f32[1,4,16,128]{3,2,1,0:T(8,128)S(1)} custom-call(bf16[16,16,128]{2,1,0:T(8,128)(2,1)} %vol_hbm.1, s32[8,8,64]{2,1,0:T(8,128)} %lab_hbm.1, s32[4,4]{1,0:T(4,128)} %order_hbm.1, s32[4]{0:T(128)} %shear_hbm.1, s32[16]{0:T(128)} %tf_hbm.1, f32[4,256]{1,0:T(4,128)} %bitcast.1), custom_call_target="tpu_custom_call" | custom-call | tf_op jit(solution)/shard_map/pallas_call | solution.py:309
  10.2 0.6 %copy.8 = f32[1,4,16,128]{3,2,1,0:T(8,128)} copy(f32[1,4,16,128]{3,2,1,0:T(8,128)S(1)} %shard_map.64) | data formatting | bytes 65536

commit v4 on v3

--- a/solution.py
+++ b/solution.py
@@ -48,6 +48,7 @@
     part_send,
     part_recv,
     load_sem,
+    ready_sem,
 ):
     brick_x, brick_y, cells_z = vol_ref.shape
     half_x, half_y, half_z = lab_ref.shape
@@ -63,10 +64,6 @@
     for step in range(1, bricks):
         other = lax.rem(me + step, bricks)
         pl.semaphore_signal(barrier, inc=1, device_id={"bx": other}, device_id_type=MESH)
-
-    @pl.when(has_up)
-    def _():
-        pl.semaphore_signal(barrier, inc=1, device_id={"by": col - 1}, device_id_type=MESH)
 
     @pl.when(has_down)
     def _():
@@ -86,8 +83,18 @@
     ]
     for load in loads:
         load.start()
-    amount = bricks - 1 + has_up.astype(jnp.int32) + has_down.astype(jnp.int32)
+    loads[0].wait()
+    for x in range(brick_x):
+        plane = vol_ref[x].astype(jnp.float32)
+        edge_ref[0, x : x + 1, :] = plane[brick_y - 1 :, :]
+        edge_ref[1, x : x + 1, :] = plane[:1, :]
+
+    amount = bricks - 1 + has_up.astype(jnp.int32)
     pl.semaphore_wait(barrier, amount)
+
+    @pl.when(has_up)
+    def _():
+        pl.semaphore_signal(ready_sem, inc=1, device_id={"by": col - 1}, device_id_type=MESH)
 
     def copy(index, src, dst, target):
         return pltpu.make_async_remote_copy(
@@ -105,15 +112,14 @@
         (copy(2, edge_ref.at[0], row_ref.at[0], {"by": col + 1}), has_down, has_up, row_ref, 0),
         (copy(3, edge_ref.at[1], row_ref.at[1], {"by": col - 1}), has_up, has_down, row_ref, 1),
     )
+    pl.when(has_up)(halos[3][0].start)
     for halo, sends, receives, ref, slot in halos[:2]:
         pl.when(sends)(halo.start)
-    loads[0].wait()
-    for x in range(brick_x):
-        plane = vol_ref[x].astype(jnp.float32)
-        edge_ref[0, x : x + 1, :] = plane[brick_y - 1 :, :]
-        edge_ref[1, x : x + 1, :] = plane[:1, :]
-    for halo, sends, receives, ref, slot in halos[2:]:
-        pl.when(sends)(halo.start)
+
+    @pl.when(has_down)
+    def _():
+        pl.semaphore_wait(ready_sem, 1)
+        halos[2][0].start()
 
     for halo, sends, receives, ref, slot in halos:
 
@@ -332,6 +338,7 @@
             pltpu.SemaphoreType.DMA((views,)),
             pltpu.SemaphoreType.DMA((bricks, per_dev)),
             pltpu.SemaphoreType.DMA((6,)),
+            pltpu.SemaphoreType.REGULAR,
         ],
         compiler_params=pltpu.CompilerParams(
             collective_id=0, has_side_effects=True, vmem_limit_bytes=32 * 2**20

time: 11 us -> 10.3 us (0.936)
  Pallas kernels: 10.2 us -> 9.52 us
    pallas_call x1, Pallas kernels: 10.2 us -> 9.52 us  [on_device(): pl.pallas_call(functools.partial(render, bricks, columns), out_shape=jax....]
where the time goes in v4:
time: 10.3 us; the launch traced here: 10.1 us
  Pallas kernels  9.52 us (92%)
  local copies, waits for them, and re-layouts  0.62 us (6%)
    pallas_call x1, Pallas kernels, on_device(): pl.pallas_call(functools.partial(render, bricks, columns), out_shape=jax....  9.52 us
    unnamed x1, local copies, waits for them, and re-layouts  0.62 us

profile of v4, /device:TPU:0, one launch (start us, length us, event | category | flops | bytes accessed | tf_op | source)
XLA Modules:
  0.0 10.1 jit_solution(14302604900668351081)
XLA Ops:
  0.0 9.5 %shard_map.64 = f32[1,4,16,128]{3,2,1,0:T(8,128)S(1)} custom-call(bf16[16,16,128]{2,1,0:T(8,128)(2,1)} %vol_hbm.1, s32[8,8,64]{2,1,0:T(8,128)} %lab_hbm.1, s32[4,4]{1,0:T(4,128)} %order_hbm.1, s32[4]{0:T(128)} %shear_hbm.1, s32[16]{0:T(128)} %tf_hbm.1, f32[4,256]{1,0:T(4,128)} %bitcast.1), custom_call_target="tpu_custom_call" | custom-call | tf_op jit(solution)/shard_map/pallas_call | solution.py:315
  9.5 0.6 %copy.8 = f32[1,4,16,128]{3,2,1,0:T(8,128)} copy(f32[1,4,16,128]{3,2,1,0:T(8,128)S(1)} %shard_map.64) | data formatting | bytes 65536

commit v5 on v4

--- a/solution.py
+++ b/solution.py
@@ -183,26 +183,28 @@
             grad_x = (dens(x + 1) - dens(x - 1)) * 0.5
             grad_sq = grad_sq + grad_x * grad_x
         grad_ref[x] = grad_sq
-        glow_ref[x] = 1.0 / (1.0 + jnp.exp(-2.0 * centre))
+        glow = 1.0 / (1.0 + jnp.exp(-2.0 * centre))
+        glow_ref[x] = glow
+        field_ref[x, 3] = 6.0 / x_cells * glow * rgbo_ref[x // 2, 3]
+        above = jnp.where(row == 0, 0.0, pltpu.roll(centre, 1, 0))
+        below = jnp.where(row == brick_y - 1, 0.0, pltpu.roll(centre, brick_y - 1, 0))
+        field_ref[x, 0] = below - above
 
     for halo, sends, receives, ref, slot in halos:
         pl.when(receives)(halo.wait_recv)
 
     for x in range(brick_x):
-        centre = dens(x)
         grad_sq = grad_ref[x]
         if x == 0 or x == brick_x - 1:
             grad_x = (dens(x + 1) - dens(x - 1)) * 0.5
             grad_sq = grad_sq + grad_x * grad_x
-        above = jnp.where(row == 0, row_ref[0, x : x + 1, :], pltpu.roll(centre, 1, 0))
-        below = jnp.where(
-            row == brick_y - 1, row_ref[1, x : x + 1, :], pltpu.roll(centre, brick_y - 1, 0)
-        )
-        grad_y = (below - above) * 0.5
+        above = jnp.where(row == 0, row_ref[0, x : x + 1, :], 0.0)
+        below = jnp.where(row == brick_y - 1, row_ref[1, x : x + 1, :], 0.0)
+        grad_y = (field_ref[x, 0] + below - above) * 0.5
         grad_sq = grad_sq + grad_y * grad_y
         edge = grad_sq / (1.0 + grad_sq)
         glow = glow_ref[x]
-        tau = 6.0 / x_cells * glow * rgbo_ref[x // 2, 3] * (0.25 + edge)
+        tau = field_ref[x, 3] * (0.25 + edge)
         gain = one_minus_exp(tau) * glow
         for chan in range(3):
             field_ref[x, chan] = gain * rgbo_ref[x // 2, chan]

time: 10.3 us -> 10.3 us (level)
  no operation moved by 1% of the time
where the time goes in v5:
time: 10.3 us; the launch traced here: 10.1 us
  Pallas kernels  9.5 us (92%)
  local copies, waits for them, and re-layouts  0.62 us (6%)
    pallas_call x1, Pallas kernels, on_device(): pl.pallas_call(functools.partial(render, bricks, columns), out_shape=jax....  9.5 us
    unnamed x1, local copies, waits for them, and re-layouts  0.62 us

profile of v5, /device:TPU:0, one launch (start us, length us, event | category | flops | bytes accessed | tf_op | source)
XLA Modules:
  0.0 10.1 jit_solution(9107555524494571074)
XLA Ops:
  0.0 9.5 %shard_map.64 = f32[1,4,16,128]{3,2,1,0:T(8,128)S(1)} custom-call(bf16[16,16,128]{2,1,0:T(8,128)(2,1)} %vol_hbm.1, s32[8,8,64]{2,1,0:T(8,128)} %lab_hbm.1, s32[4,4]{1,0:T(4,128)} %order_hbm.1, s32[4]{0:T(128)} %shear_hbm.1, s32[16]{0:T(128)} %tf_hbm.1, f32[4,256]{1,0:T(4,128)} %bitcast.1), custom_call_target="tpu_custom_call" | custom-call | tf_op jit(solution)/shard_map/pallas_call | solution.py:317
  9.5 0.6 %copy.8 = f32[1,4,16,128]{3,2,1,0:T(8,128)} copy(f32[1,4,16,128]{3,2,1,0:T(8,128)S(1)} %shard_map.64) | data formatting | bytes 65536
